TPU v7x, 32 devices: a whole 2x2x4 slice. The times are simulated.
32 devices in a mesh: tm: 8 (over z, y), chan: 4 (over x, core).
Axes of the slice: x: 2, y: 2, z: 4, core: 2. Of those that a mesh axis runs over, the one named last changes fastest.
Arguments:
- record: bfloat16 [28672, 10240], P('tm', 'chan'), may hold values from -256 to 256
- pilot_sweep: bfloat16 [3072], replicated, may hold values from -0.109375 to 0.109375
- sweep_table: int32 [3, 8], replicated, may hold values from 0 to 28671, as said below
- owner_map: int32 [2], replicated, may hold values from 0 to 1, each once
Outputs:
- stacks: float32 [2, 1024, 10240], P(None, 'tm', 'chan')
Inputs may be any that keep to these rules, and one draw needn't show every extreme that they name: `sweep_table`: column g is sweep g: row 0 lies in [3584 g, 3584 g + 512]; row 1 is its shot, and every shot has at least one sweep; row 2 is the number of earlier sweeps with the same shot.
All inputs are finite; a program needn't handle non-finite values.
Results may differ from a plain program's by a relative error of at most 0.0029.
Values may be sent and summed in bfloat16 or wider, within the bound.
A program may use at most 128 MiB of HBM per device.

v0:
```python
import jax
import jax.numpy as jnp
from jax import lax
from jax.sharding import PartitionSpec as P

SEG = 1024
ITERS = 3


EPSILON = 1e-06


def passed_along(value, axis, steps):
    count = lax.axis_size(axis)
    first, last = (max(0, -steps), min(count, count - steps))
    return lax.ppermute(value, axis, [(source, source + steps) for source in range(first, last)])


def toeplitz_matrix(pilot_sweep, out_rows, width):
    length = pilot_sweep.shape[0]
    padded = jnp.concatenate([pilot_sweep, jnp.zeros((width + 1 - length,), pilot_sweep.dtype)])
    tiled = jnp.tile(padded, out_rows)[: out_rows * width]
    return tiled.reshape(out_rows, width)


def shards(record, pilot_sweep, sweep_table, owner_map):
    block_rows, channels = record.shape
    listen = SEG
    width = listen + pilot_sweep.shape[0]
    following = passed_along(record[:listen], "tm", -1)
    joined = jnp.concatenate([record, following], axis=0)
    here = lax.axis_index("tm")
    column = lax.dynamic_slice_in_dim(sweep_table, here, 1, 1)[:, 0]
    offset = column[0] - here * block_rows
    window = lax.dynamic_slice_in_dim(joined, offset, width, 0)
    correlation = jnp.dot(
        toeplitz_matrix(pilot_sweep, listen, width), window, preferred_element_type=jnp.float32
    )
    polarity = 1.0 - 2.0 * (column[2] % 2).astype(jnp.float32)
    traces = (correlation * polarity).astype(jnp.bfloat16)[None]
    arrived = lax.all_to_all(traces, "tm", split_axis=1, concat_axis=0, tiled=True)
    sweep_count, rows_here = (arrived.shape[0], arrived.shape[1])
    shot_count = owner_map.shape[0]
    member = (sweep_table[1][:, None] == jnp.arange(shot_count, dtype=jnp.int32)[None, :]).astype(
        jnp.float32
    )
    counts = jnp.sum(member, axis=0)
    flat = arrived.reshape(sweep_count, rows_here * channels)
    summed = jnp.dot(member.astype(jnp.bfloat16).T, flat, preferred_element_type=jnp.float32)
    stacked = (summed / counts[:, None]).reshape(shot_count, rows_here, channels)
    samples = arrived.astype(jnp.float32)
    total_count = sweep_count * channels * lax.axis_size("chan")
    for iteration in range(ITERS):
        fitted = jnp.einsum("gk,kuc->guc", member, stacked, precision=lax.Precision.HIGHEST)
        partial_energy = jnp.sum(jnp.square(samples - fitted), axis=1)
        energy_sum = lax.psum(partial_energy, "tm")
        everything = lax.psum(jnp.sum(energy_sum), "chan")
        energy = energy_sum / listen
        spread = everything / (listen * total_count) + EPSILON
        weight = 1.0 / (1.0 + energy / spread)
        weighted = weight[:, None, :] * samples
        numerator = jnp.einsum("gk,guc->kuc", member, weighted, precision=lax.Precision.HIGHEST)
        denominator = jnp.dot(member.T, weight, precision=lax.Precision.HIGHEST)
        stacked = numerator / denominator[:, None, :]
    return jnp.zeros_like(stacked).at[owner_map].set(stacked)


def solution(mesh):
    placed = (P("tm", "chan"), P(), P(), P())
    return jax.shard_map(
        shards, mesh=mesh, in_specs=placed, out_specs=P(None, "tm", "chan"), check_vma=False
    )
```

profile of v0, /device:TPU:0, one launch (start us, length us, event | category | flops | bytes accessed | tf_op | source)
XLA Modules:
  0.0 786.9 jit_solution(9013679591784072137)
XLA Ops:
  6.5 5.2 slice.19
  11.7 1.3 collective-permute-start
  13.0 0.1 constant_dynamic-slice_fusion
  13.1 0.6 fusion.42
  16.4 4.0 tile.4
  20.4 17.4 %tile.10 = bf16[4195328]{0:T(1024)(128)(2,1)} reshape(bf16[1024,4097]{1,0:T(8,128)(2,1)} %tile.4) | data formatting | bytes 16781312 | tf_op jit(solution)/shard_map/tile | solution.py:22
  37.8 7.3 slice.22
  45.0 13.3 %reshape.28 = bf16[1024,4096]{1,0:T(8,128)(2,1)} reshape(bf16[4194304]{0:T(1024)(128)(2,1)} %slice.22) | data formatting | bytes 16777216 | tf_op jit(solution)/shard_map/reshape | solution.py:23
  58.4 71.6 %collective-permute-done = bf16[1024,2560]{1,0:T(8,128)(2,1)} collective-permute-done((bf16[1024,2560]{1,0:T(8,128)(2,1)}, bf16[1024,2560]{1,0:T(8,128)(2,1)}, u32[]{:S(2)}, u32[]{:S(2)}) %collective-permute-start) | collective-permute-done | bytes 5242912 | tf_op jit(solution)/shard_map/ppermute | solution.py:16
  129.9 28.0 %fusion.11 = bf16[1,1024,2560]{2,1,0:T(8,128)(2,1)S(1)} fusion(f32[]{:T(128)S(6)} %sub.16, bf16[1024,4096]{1,0:T(8,128)(2,1)} %reshape.28, s32[]{:T(128)S(6)} %select_n.18, bf16[3584,2560]{1,0:T(8,128)(2,1)} %param.4, bf16[1024,2560]{1,0:T(8,128)(2,1)} %collective-permute-done), kind=kOutput, calls=%fused_computation.19 | convolution fusion | flops 21522022400 | bytes 37224456 | tf_op jit(solution)/shard_map/dot_general | solution.py:36
  158.0 57.9 %copy.41 = bf16[1,1024,2560]{2,0,1:T(2,128)(2,1)} copy(bf16[1,1024,2560]{2,1,0:T(8,128)(2,1)S(1)} %fusion.11) | data formatting | bytes 10485760 | tf_op jit(solution)/shard_map/broadcast_in_dim | solution.py:40
  215.8 0.5 broadcast.39
  216.3 35.2 %reduce.2 = bf16[1024,2560]{1,0:T(8,128)(2,1)} reduce(bf16[1024,1,2560]{2,1,0:T(2,128)(2,1)} %bitcast.44, bf16[]{:T(256)} %broadcast.39), dimensions={1}, to_apply=%bitcast.32.reduce_sub_computation | reduce | bytes 10485762
  251.5 8.6 %reshape.43 = bf16[8,2,163840]{2,1,0:T(2,128)(2,1)} reshape(bf16[1024,2560]{1,0:T(8,128)(2,1)} %reduce.2) | data formatting | bytes 10485760
  260.1 5.9 all-to-all-start
  266.0 0.0 all-reduce.5.cloned.1.call-start
  266.0 0.1 convert_reduce_fusion
  266.1 114.7 %all-to-all-done = bf16[8,2,163840]{2,1,0:T(2,128)(2,1)} async-done(((bf16[8,2,163840]{2,1,0:T(2,128)(2,1)}), bf16[8,2,163840]{2,1,0:T(2,128)(2,1)}, u32[]{:S(2)}, u32[]{:S(2)}) %all-to-all-start) | async-done | bytes 5242912 | tf_op jit(solution)/shard_map/all_to_all | solution.py:41
  380.8 10.0 %reshape.44 = bf16[1024,1,2560]{2,1,0:T(2,128)(2,1)} reshape(bf16[8,2,163840]{2,1,0:T(2,128)(2,1)} %all-to-all-done) | data formatting | bytes 10485760
  390.8 34.5 %bitcast_reduce_fusion = bf16[1024,2560]{1,0:T(8,128)(2,1)} fusion(bf16[1024,1,2560]{2,1,0:T(2,128)(2,1)} %reshape.44), kind=kLoop, calls=%fused_computation.57 | loop fusion | bytes 10485760 | tf_op jit(solution)/shard_map/all_to_all | solution.py:41
  425.3 5.3 copy.20
  430.7 2.3 copy-done
  433.0 5.4 convert.1
  438.4 7.3 reshape.29
  445.7 4.1 convolution_divide_fusion
  449.9 0.9 slice-done.2
  450.7 12.7 %multiply_reduce_fusion.2 = f32[8,2560]{1,0:T(8,128)} fusion(f32[8,128,2560]{2,1,0:T(8,128)S(1)} %bitcast.39, f32[2,128,2560]{2,0,1:T(2,128)S(1)} %bitcast.45, s32[8]{0:T(128)S(1)} %slice_bitcast_fusion), kind=kOutput, calls=%fused_computation.14 | convolution fusion | flops 70758416 | bytes 13189152 | tf_op jit(solution)/shard_map/gk,kuc->guc/dot_general | solution.py:54
  463.4 0.0 all-reduce.5.cloned.1.call-update
  463.4 0.0 all-reduce.7.cloned.1.call-start
  463.5 67.9 %all-reduce.5.cloned.1.call-done = f32[8,2560]{1,0:T(8,128)} async-done(((f32[8,2560]{1,0:T(8,128)}), f32[8,2560]{1,0:T(8,128)}) %all-reduce.5.cloned.1.call-update) | async-done | bytes 81936 | tf_op jit(solution)/shard_map/psum | solution.py:56
  531.4 1.5 reduce_sum.65
  532.9 6.7 psum.43
  540.3 0.9 add_divide_fusion.2
  541.2 0.0 slice-start.3
  541.2 0.0 slice-start.4
  541.2 4.1 convert_multiply_fusion.2
  545.3 0.2 fusion.28
  545.5 10.8 %fusion.7 = f32[2,128,2560]{2,0,1:T(2,128)} fusion(f32[8,128,2560]{2,1,0:T(8,128)S(1)} %convert_multiply_fusion.2, s32[8]{0:T(128)S(1)} %slice_bitcast_fusion), kind=kOutput, calls=%fused_computation.10 | convolution fusion | flops 62914576 | bytes 13107232 | tf_op jit(solution)/shard_map/gk,guc->kuc/dot_general | solution.py:62
  556.3 15.5 %multiply_reduce_fusion.1 = f32[8,2560]{1,0:T(8,128)} fusion(f32[8,128,2560]{2,1,0:T(8,128)S(1)} %bitcast.41, f32[2,128,2560]{2,0,1:T(2,128)} %fusion.7, f32[2,2560]{1,0:T(2,128)S(1)} %fusion.28, s32[8]{0:T(128)S(1)} %slice_bitcast_fusion), kind=kOutput, calls=%fused_computation.13 | convolution fusion | flops 71413776 | bytes 13209632 | tf_op jit(solution)/shard_map/gk,kuc->guc/dot_general | solution.py:54
  571.8 0.0 all-reduce.7.cloned.1.call-update
  571.8 0.0 all-reduce.9.cloned.1.call-start
  571.9 68.8 %all-reduce.7.cloned.1.call-done = f32[8,2560]{1,0:T(8,128)} async-done(((f32[8,2560]{1,0:T(8,128)}), f32[8,2560]{1,0:T(8,128)}) %all-reduce.7.cloned.1.call-update) | async-done | bytes 81936 | tf_op jit(solution)/shard_map/psum | solution.py:56
  640.7 1.5 reduce_sum.67
  642.2 6.5 psum.45
  649.3 0.9 add_divide_fusion.1
  650.2 0.0 slice-start.6
  650.3 0.0 slice-start.7
  650.3 4.1 convert_multiply_fusion
  654.4 0.2 fusion.27
  654.5 0.0 slice-start.8
  654.5 10.8 %fusion.5 = f32[2,128,2560]{2,0,1:T(2,128)} fusion(f32[8,128,2560]{2,1,0:T(8,128)S(1)} %convert_multiply_fusion, s32[8]{0:T(128)S(1)} %slice_bitcast_fusion), kind=kOutput, calls=%fused_computation.8 | convolution fusion | flops 62914576 | bytes 13107232 | tf_op jit(solution)/shard_map/gk,guc->kuc/dot_general | solution.py:62
  665.4 0.0 copy-start.3
  665.4 15.6 %multiply_reduce_fusion = f32[8,2560]{1,0:T(8,128)} fusion(f32[8,128,2560]{2,1,0:T(8,128)S(1)} %bitcast.43, f32[2,128,2560]{2,0,1:T(2,128)} %fusion.5, f32[2,2560]{1,0:T(2,128)S(1)} %fusion.27, s32[8]{0:T(128)S(1)} %slice_bitcast_fusion), kind=kOutput, calls=%fused_computation.12 | convolution fusion | flops 71413776 | bytes 13209632 | tf_op jit(solution)/shard_map/gk,kuc->guc/dot_general | solution.py:54
  681.0 0.0 all-reduce.9.cloned.1.call-update
  681.0 68.9 %all-reduce.9.cloned.1.call-done = f32[8,2560]{1,0:T(8,128)} async-done(((f32[8,2560]{1,0:T(8,128)}), f32[8,2560]{1,0:T(8,128)}) %all-reduce.9.cloned.1.call-update) | async-done | bytes 81936 | tf_op jit(solution)/shard_map/psum | solution.py:56
  749.9 1.5 reduce_sum.69
  751.4 6.6 psum.47
  758.6 0.9 add_divide_fusion
  759.5 3.9 convert_multiply_fusion.1
  763.5 0.2 fusion.29
  763.6 10.0 %fusion.16 = f32[2,128,2560]{2,0,1:T(2,128)S(1)} fusion(f32[8,128,2560]{2,1,0:T(8,128)S(1)} %convert_multiply_fusion.1, f32[2,2560]{1,0:T(2,128)S(1)} %fusion.29, s32[8]{0:T(128)S(1)} %slice_bitcast_fusion), kind=kOutput, calls=%fused_computation.22 | convolution fusion | flops 63569936 | bytes 13127712 | tf_op jit(solution)/shard_map/gk,guc->kuc/dot_general | solution.py:62
  773.6 0.5 copy.28
  774.1 1.8 broadcast_in_dim.6
  775.9 3.9 scatter_fusion
  (24 shorter events, 0.0 us)
Async XLA Ops:
  6.5 6.5 copy-start.2
  6.5 9.8 %copy-start.1 = (bf16[3072]{0:T(1024)(128)(2,1)S(1)}, bf16[3072]{0:T(1024)(128)(2,1)}, u32[]{:S(2)}) copy-start(bf16[3072]{0:T(1024)(128)(2,1)} %param.5) | copy-start | bytes 18436
  11.7 118.2 %collective-permute-start = (bf16[1024,2560]{1,0:T(8,128)(2,1)}, bf16[1024,2560]{1,0:T(8,128)(2,1)}, u32[]{:S(2)}, u32[]{:S(2)}) collective-permute-start(bf16[1024,2560]{1,0:T(8,128)(2,1)} %slice.19), channel_id=1, source_target_pairs={{4,0},{8,4},{12,8},{16,12},{20,16},{24,20},{28,24},{5,1},{9,5},{13... | collective-permute-start | bytes 15728648 | tf_op jit(solution)/shard_map/ppermute | solution.py:16
  260.1 120.8 %all-to-all-start = ((bf16[8,2,163840]{2,1,0:T(2,128)(2,1)}), bf16[8,2,163840]{2,1,0:T(2,128)(2,1)}, u32[]{:S(2)}, u32[]{:S(2)}) async-start(bf16[8,2,163840]{2,1,0:T(2,128)(2,1)} %reshape.43), calls=%async_computation | async-start | bytes 10485760 | tf_op jit(solution)/shard_map/all_to_all | solution.py:41
  266.0 265.4 %all-reduce.5.cloned.1.call-start = ((), (), s32[]{:S(2)}) async-start(), calls=%async_computation.1 | async-start | bytes 163840 | tf_op jit(solution)/shard_map/psum | solution.py:56
  430.7 2.3 copy-start
  438.4 11.5 %slice-start = ((s8[10485760]{0:T(1024)(128)(4,1)}), s8[2097152]{0:T(1024)(128)(4,1)S(1)}, s32[]{:S(2)}) async-start(s8[10485760]{0:T(1024)(128)(4,1)} %bitcast.38), calls=%async_computation.4 | async-start | bytes 4194304
  445.7 4.2 slice-start.1
  445.7 5.0 slice-start.2
  463.4 177.3 %all-reduce.7.cloned.1.call-start = ((), (), s32[]{:S(2)}) async-start(), calls=%async_computation.2 | async-start | bytes 163840 | tf_op jit(solution)/shard_map/psum | solution.py:56
  541.2 15.1 %slice-start.3 = ((s8[10485760]{0:T(1024)(128)(4,1)}), s8[4194304]{0:T(1024)(128)(4,1)S(1)}, s32[]{:S(2)}) async-start(s8[10485760]{0:T(1024)(128)(4,1)} %bitcast.40), calls=%async_computation.7 | async-start | bytes 8388608
  541.2 15.1 %slice-start.4 = ((s8[10485760]{0:T(1024)(128)(4,1)}), s8[4194304]{0:T(1024)(128)(4,1)S(1)}, s32[]{:S(2)}) async-start(s8[10485760]{0:T(1024)(128)(4,1)} %bitcast.40), calls=%async_computation.8 | async-start | bytes 8388608
  545.5 10.8 %slice-start.5 = ((s8[10485760]{0:T(1024)(128)(4,1)}), s8[2097152]{0:T(1024)(128)(4,1)S(1)}, s32[]{:S(2)}) async-start(s8[10485760]{0:T(1024)(128)(4,1)} %bitcast.40), calls=%async_computation.9 | async-start | bytes 4194304
  571.8 178.1 %all-reduce.9.cloned.1.call-start = ((), (), s32[]{:S(2)}) async-start(), calls=%async_computation.3 | async-start | bytes 163840 | tf_op jit(solution)/shard_map/psum | solution.py:56
  650.2 15.1 %slice-start.6 = ((s8[10485760]{0:T(1024)(128)(4,1)}), s8[4194304]{0:T(1024)(128)(4,1)S(1)}, s32[]{:S(2)}) async-start(s8[10485760]{0:T(1024)(128)(4,1)} %bitcast.42), calls=%async_computation.10 | async-start | bytes 8388608
  650.3 15.1 %slice-start.7 = ((s8[10485760]{0:T(1024)(128)(4,1)}), s8[4194304]{0:T(1024)(128)(4,1)S(1)}, s32[]{:S(2)}) async-start(s8[10485760]{0:T(1024)(128)(4,1)} %bitcast.42), calls=%async_computation.11 | async-start | bytes 8388608
  654.5 10.8 %slice-start.8 = ((s8[10485760]{0:T(1024)(128)(4,1)}), s8[2097152]{0:T(1024)(128)(4,1)S(1)}, s32[]{:S(2)}) async-start(s8[10485760]{0:T(1024)(128)(4,1)} %bitcast.42), calls=%async_computation.12 | async-start | bytes 4194304
  665.4 86.0 %copy-start.3 = (s32[2]{0:T(128)S(1)}, s32[2]{0:T(128)}, u32[]{:S(2)}) copy-start(s32[2]{0:T(128)} %param.7) | copy-start | bytes 28
Sparse Core Ops, SparseCore 0:
  463.5 67.7 all-reduce.4
  571.9 68.7 all-reduce.6
  681.1 68.7 all-reduce.8
where the time goes:
time: 797 us; the launch traced here: 787 us
  waiting for transfers between devices  392 us (49%)
  local copies, waits for them, and re-layouts  181 us (23%)
  matrix products  108 us (14%)
  other arithmetic  60 us (8%)
  blocking collectives  19.8 us (2%)
  between operations  18.5 us (2%)
    psum x3, waiting for transfers between devices, shards(): energy_sum = lax.psum(partial_energy, 'tm')  206 us
    all_to_all x1, waiting for transfers between devices, shards(): lax.all_to_all(traces, 'tm', split_axis=1, concat_axis=0, tiled=True)  115 us
    ppermute x1, waiting for transfers between devices, passed_along(): lax.ppermute(value, axis, [(source, source + steps) for source in range(f...  71.6 us
    broadcast_in_dim x1, local copies, waits for them, and re-layouts, shards(): traces = (correlation * polarity).astype(jnp.bfloat16)[None]  57.9 us
    dot_general x3, matrix products, shards(): jnp.einsum('gk,kuc->guc', member, stacked, precision=lax.Precision.HIGHEST)  43.7 us
    all_to_all x2, local copies, waits for them, and re-layouts, shards(): lax.all_to_all(traces, 'tm', split_axis=1, concat_axis=0, tiled=True)  39.8 us
    unnamed x4, other arithmetic  35.2 us
    dot_general x3, matrix products, shards(): jnp.einsum('gk,guc->kuc', member, weighted, precision=lax.Precision.HIGHEST)  31.6 us
  transfers between devices with their start and end apart: 5, of which 5 were waited for; matrix products, arithmetic and copies ran while one was open for 5% of the time, Pallas kernels for 0%

commit v1 on v0

v1 whole, which is shorter than its diff:
```python
import functools

import jax
import jax.numpy as jnp
from jax import lax
from jax.experimental import pallas as pl
from jax.experimental.pallas import tpu as pltpu
from jax.sharding import PartitionSpec as P

SEG = 1024
ITERS = 3
EPSILON = 1e-06
MESH = pl.DeviceIdType.MESH
LANES = 128


def passed_along(value, axis, steps):
    count = lax.axis_size(axis)
    first, last = (max(0, -steps), min(count, count - steps))
    return lax.ppermute(value, axis, [(source, source + steps) for source in range(first, last)])


def template_kernel(offset_ref, pilot_ref, out_ref):
    rows, width = out_ref.shape
    offset = offset_ref[0]
    base = jnp.broadcast_to(pilot_ref[...], (8, width))
    base = pltpu.roll(base, 0, 1, stride=1, stride_axis=0)

    @pl.loop(0, rows // 16)
    def _(group):
        shift = offset + group * 16
        first = pltpu.roll(base, shift, 1)
        second = pltpu.roll(base, shift + 8, 1)
        block = jnp.concatenate([first, second], axis=0)
        out_ref[pl.ds(pl.multiple_of(group * 16, 16), 16), :] = block.astype(out_ref.dtype)


def template(pilot_sweep, offset, rows, slack):
    length = pilot_sweep.shape[0]
    width = length + slack + rows
    padded = jnp.pad(pilot_sweep.astype(jnp.float32), (0, width - length))[None, :]
    return pl.pallas_call(
        template_kernel,
        out_shape=jax.ShapeDtypeStruct((rows, width), jnp.bfloat16),
        in_specs=[
            pl.BlockSpec(memory_space=pltpu.SMEM),
            pl.BlockSpec(memory_space=pltpu.VMEM),
        ],
        out_specs=pl.BlockSpec(memory_space=pltpu.VMEM),
        name="template",
    )(offset.reshape(1), padded)


def stack_kernel(
    n_tm, n_chan, total_count,
    traces, same, place, out,
    dpart, rsbuf, dall, coef, tiles,
    rs_send, rs_recv, ag_send, ag_recv, en_send, en_recv,
):
    sweeps, rows, channels = traces.shape
    shots = out.shape[0]
    half_pairs = sweeps // 2
    half = channels // 2
    t = lax.axis_index("tm")
    c = lax.axis_index("chan")

    barrier = pltpu.get_barrier_semaphore()
    for k in range(1, n_tm):
        pl.semaphore_signal(barrier, inc=1, device_id=(lax.rem(t + k, n_tm), c), device_id_type=MESH)
    for k in range(1, n_chan):
        pl.semaphore_signal(barrier, inc=1, device_id=(t, lax.rem(c + k, n_chan)), device_id_type=MESH)

    def sample(g, start, lanes):
        return traces[g, pl.ds(start, 16), lanes].astype(jnp.float32)

    for side in range(2):

        @pl.loop(0, half // LANES)
        def _(chunk):
            lanes = pl.ds(pl.multiple_of(side * half + chunk * LANES, LANES), LANES)
            inner = pl.ds(pl.multiple_of(chunk * LANES, LANES), LANES)

            group = sweeps if sweeps <= 8 else 2
            for g0 in range(0, sweeps, group):
                totals = {}
                for start in range(0, rows, 16):
                    held = {}
                    for g in range(g0, g0 + group):
                        for d in range(1, half_pairs + 1):
                            if d == half_pairs and g >= half_pairs:
                                continue
                            ends = (g, (g + d) % sweeps)
                            for end in ends:
                                if end not in held:
                                    held[end] = sample(end, start, lanes)
                            gap = held[ends[0]] - held[ends[1]]
                            gap = gap * gap
                            gap = gap[:8] + gap[8:]
                            totals[g, d] = totals[g, d] + gap if start else gap
                for (g, d), total in totals.items():
                    row = jnp.sum(total, axis=0, keepdims=True)
                    dpart[2 * d - 2 + side, g:g + 1, inner] = row
                    if d == half_pairs:
                        dpart[2 * d - 2 + side, g + d:g + d + 1, inner] = row

    pl.semaphore_wait(barrier, n_tm - 1 + n_chan - 1)

    def rs_copy(k):
        peer = lax.rem(t + k, n_tm)
        return pltpu.make_async_remote_copy(
            src_ref=dpart.at[peer], dst_ref=rsbuf.at[t],
            send_sem=rs_send.at[peer], recv_sem=rs_recv.at[t],
            device_id=(peer, c), device_id_type=MESH,
        )

    def rs_arrival(k):
        peer = lax.rem(t + k, n_tm)
        return pltpu.make_async_remote_copy(
            src_ref=dpart.at[peer], dst_ref=rsbuf.at[peer],
            send_sem=rs_send.at[peer], recv_sem=rs_recv.at[peer],
            device_id=(peer, c), device_id_type=MESH,
        )

    for k in range(1, n_tm):
        rs_copy(k).start()
    rsbuf[t] = dpart[t]
    for k in range(1, n_tm):
        rs_arrival(k).wait_recv()
    total = rsbuf[0]
    for k in range(1, n_tm):
        total = total + rsbuf[k]
    dall[t] = total

    def ag_copy(k):
        peer = lax.rem(t + k, n_tm)
        return pltpu.make_async_remote_copy(
            src_ref=dall.at[t], dst_ref=dall.at[t],
            send_sem=ag_send.at[peer], recv_sem=ag_recv.at[t],
            device_id=(peer, c), device_id_type=MESH,
        )

    def ag_arrival(k):
        peer = lax.rem(t + k, n_tm)
        return pltpu.make_async_remote_copy(
            src_ref=dall.at[peer], dst_ref=dall.at[peer],
            send_sem=ag_send.at[peer], recv_sem=ag_recv.at[peer],
            device_id=(peer, c), device_id_type=MESH,
        )

    for k in range(1, n_tm):
        ag_copy(k).start()
    for k in range(1, n_tm):
        ag_arrival(k).wait_recv()

    masks = [same[d][:, 0:1] for d in range(half_pairs)]

    def ahead(value, d):
        return pltpu.roll(value, sweeps - d, 0)

    def behind(value, d):
        return pltpu.roll(value, d, 0)

    def over_shot(value):
        result = value
        for d in range(1, half_pairs + 1):
            result = result + masks[d - 1] * ahead(value, d)
            if d < half_pairs:
                result = result + behind(masks[d - 1] * value, d)
        return result

    def pair(d, side):
        return masks[d - 1] * dall[2 * (d - 1) + side]

    def energy_of(weight, side):
        spent = jnp.zeros_like(weight)
        for d in range(1, half_pairs + 1):
            gaps = pair(d, side)
            spent = spent + gaps * ahead(weight, d)
            if d < half_pairs:
                spent = spent + behind(gaps * weight, d)
        scale = 1.0 / over_shot(weight)
        energy = spent * scale - 0.5 * over_shot(weight * spent) * (scale * scale)
        return jnp.maximum(energy, 0.0) / SEG

    weights = [jnp.ones((sweeps, half), jnp.float32) for _ in range(2)]
    for iteration in range(ITERS):
        energies = [energy_of(weights[side], side) for side in range(2)]
        part = jnp.zeros((sweeps, LANES), jnp.float32)
        for side in range(2):
            for chunk in range(half // LANES):
                part = part + energies[side][:, chunk * LANES:(chunk + 1) * LANES]
        tiles[iteration, c] = part

        def en_copy(k, iteration=iteration):
            peer = lax.rem(c + k, n_chan)
            return pltpu.make_async_remote_copy(
                src_ref=tiles.at[iteration, c], dst_ref=tiles.at[iteration, c],
                send_sem=en_send.at[iteration, peer], recv_sem=en_recv.at[iteration, c],
                device_id=(t, peer), device_id_type=MESH,
            )

        def en_arrival(k, iteration=iteration):
            peer = lax.rem(c + k, n_chan)
            return pltpu.make_async_remote_copy(
                src_ref=tiles.at[iteration, peer], dst_ref=tiles.at[iteration, peer],
                send_sem=en_send.at[iteration, peer], recv_sem=en_recv.at[iteration, peer],
                device_id=(t, peer), device_id_type=MESH,
            )

        for k in range(1, n_chan):
            en_copy(k).start()
        for k in range(1, n_chan):
            en_arrival(k).wait_recv()
        everything = tiles[iteration, 0]
        for k in range(1, n_chan):
            everything = everything + tiles[iteration, k]
        everything = jnp.sum(jnp.sum(everything, axis=1, keepdims=True), axis=0, keepdims=True)
        spread = everything / total_count + EPSILON
        weights = [1.0 / (1.0 + energies[side] / spread) for side in range(2)]
        for k in range(1, n_chan):
            en_copy(k).wait_send()

    for side in range(2):
        share = weights[side] / over_shot(weights[side])
        for q in range(shots):
            coef[q, :, side * half:(side + 1) * half] = place[q][:, 0:1] * share

    @pl.loop(0, channels // LANES)
    def _(chunk):
        lanes = pl.ds(pl.multiple_of(chunk * LANES, LANES), LANES)
        for q0 in range(0, shots, 2):
            rates = [[coef[q, g:g + 1, lanes] for g in range(sweeps)] for q in range(q0, min(q0 + 2, shots))]

            @pl.loop(0, rows // 16)
            def _(group):
                start = pl.multiple_of(group * 16, 16)
                sums = [jnp.zeros((16, LANES), jnp.float32) for _ in rates]
                for g in range(sweeps):
                    value = sample(g, start, lanes)
                    for q, rate in enumerate(rates):
                        sums[q] = sums[q] + rate[g] * value
                for q in range(len(rates)):
                    out[q0 + q, pl.ds(start, 16), lanes] = sums[q]

    for k in range(1, n_tm):
        rs_copy(k).wait_send()
        ag_copy(k).wait_send()


def robust_stack(traces, sweep_table, owner_map):
    sweeps, rows, channels = traces.shape
    shots = owner_map.shape[0]
    n_tm, n_chan = lax.axis_size("tm"), lax.axis_size("chan")
    half_pairs = sweeps // 2
    shot = sweep_table[1]
    same = jnp.stack([shot == jnp.roll(shot, -d) for d in range(1, half_pairs + 1)])
    same = jnp.broadcast_to(same.astype(jnp.float32)[:, :, None], (half_pairs, sweeps, LANES))
    place = owner_map[shot][None, :] == jnp.arange(shots, dtype=jnp.int32)[:, None]
    place = jnp.broadcast_to(place.astype(jnp.float32)[:, :, None], (shots, sweeps, LANES))
    total_count = sweeps * channels * n_chan
    return pl.pallas_call(
        functools.partial(stack_kernel, n_tm, n_chan, total_count),
        out_shape=jax.ShapeDtypeStruct((shots, rows, channels), jnp.float32),
        in_specs=[pl.BlockSpec(memory_space=pltpu.VMEM)] * 3,
        out_specs=pl.BlockSpec(memory_space=pltpu.VMEM),
        scratch_shapes=[
            pltpu.VMEM((sweeps, sweeps, channels // 2), jnp.float32),
            pltpu.VMEM((sweeps, sweeps, channels // 2), jnp.float32),
            pltpu.VMEM((sweeps, sweeps, channels // 2), jnp.float32),
            pltpu.VMEM((shots, sweeps, channels), jnp.float32),
            pltpu.VMEM((ITERS, n_chan, sweeps, LANES), jnp.float32),
            pltpu.SemaphoreType.DMA((n_tm,)),
            pltpu.SemaphoreType.DMA((n_tm,)),
            pltpu.SemaphoreType.DMA((n_tm,)),
            pltpu.SemaphoreType.DMA((n_tm,)),
            pltpu.SemaphoreType.DMA((ITERS, n_chan)),
            pltpu.SemaphoreType.DMA((ITERS, n_chan)),
        ],
        compiler_params=pltpu.CompilerParams(
            collective_id=0, has_side_effects=True, vmem_limit_bytes=40 * 2**20
        ),
        name="robust_stack",
    )(traces, same, place)


def shards(record, pilot_sweep, sweep_table, owner_map):
    block_rows, channels = record.shape
    n_tm = lax.axis_size("tm")
    length = pilot_sweep.shape[0]
    slack = block_rows - length
    step = 256
    following = passed_along(record[:SEG], "tm", -1)
    joined = jnp.concatenate([record, following], axis=0)
    here = lax.axis_index("tm")
    column = lax.dynamic_slice_in_dim(sweep_table, here, 1, 1)[:, 0]
    offset = column[0] - here * block_rows
    polarity = 1.0 - 2.0 * (column[2] % 2).astype(jnp.float32)
    taps = template(pilot_sweep * polarity.astype(jnp.bfloat16), offset, step, slack)
    pieces = [
        jnp.dot(taps, joined[s:s + taps.shape[1]], preferred_element_type=jnp.float32).astype(jnp.bfloat16)
        for s in range(0, SEG, step)
    ]
    traces = jnp.concatenate(pieces, axis=0).reshape(n_tm, SEG // n_tm, channels)
    arrived = lax.all_to_all(traces, "tm", split_axis=0, concat_axis=0, tiled=True)
    return robust_stack(arrived, sweep_table, owner_map)


def solution(mesh):
    placed = (P("tm", "chan"), P(), P(), P())
    return jax.shard_map(
        shards, mesh=mesh, in_specs=placed, out_specs=P(None, "tm", "chan"), check_vma=False
    )
```

time: 797 us -> 329 us (0.41); the launches traced: 787 us -> 329 us
  waiting for transfers between devices: 392 us -> 206 us
  local copies, waits for them, and re-layouts: 181 us -> 30.2 us
  matrix products: 108 us -> 37.3 us
  other arithmetic: 60 us -> 4.51 us
  Pallas kernels: 0 us -> 41.2 us
  blocking collectives: 19.8 us -> 0 us
  between operations: 18.5 us -> 2.71 us
    psum x3 -> x0, waiting for transfers between devices: 206 us -> none  [shards(): energy_sum = lax.psum(partial_energy, 'tm')]
    dot_general x11 -> x4, matrix products: 108 us -> 37.3 us  [shards(): jnp.dot(taps, joined[s:s + taps.shape[1]], preferred_element_type=jnp.flo...]
    broadcast_in_dim x2 -> x3, local copies, waits for them, and re-layouts: 59.7 us -> 0.75 us  [the longest x1 0.61 us: template(): jnp.pad(pilot_sweep.astype(jnp.float32), (0, width - length))[None, :]]
    pallas_call x0 -> x2, Pallas kernels: none -> 41.2 us  [the longest x1 36.9 us: robust_stack(): pl.pallas_call(functools.partial(stack_kernel, n_tm, n_chan, total_count)...]
    all_to_all x2 -> x0, local copies, waits for them, and re-layouts: 39.8 us -> none  [shards(): lax.all_to_all(traces, 'tm', split_axis=1, concat_axis=0, tiled=True)]
    unnamed x4 -> x0, other arithmetic: 35.2 us -> none
    ppermute x1, waiting for transfers between devices: 71.6 us -> 93.1 us  [passed_along(): lax.ppermute(value, axis, [(source, source + steps) for source in range(f...]
    another operation x2 -> x0, local copies, waits for them, and re-layouts: 21.4 us -> none  [toeplitz_matrix(): tiled = jnp.tile(padded, out_rows)[:out_rows * width]]
  transfers between devices with their start and end apart: 5 -> 2, of which waited for: 5 -> 2; matrix products, arithmetic and copies ran while one was open for 5% -> 6% of each run, Pallas kernels for 0% -> 1%
where the time goes in v1:
time: 329 us
  waiting for transfers between devices  206 us (63%)
  Pallas kernels  41.2 us (13%)
  matrix products  37.3 us (11%)
  local copies, waits for them, and re-layouts  30.2 us (9%)
  starting transfers between devices  7.22 us (2%)
  other arithmetic  4.51 us (1%)
    all_to_all x1, waiting for transfers between devices, shards(): lax.all_to_all(traces, 'tm', split_axis=0, concat_axis=0, tiled=True)  113 us
    ppermute x1, waiting for transfers between devices, passed_along(): lax.ppermute(value, axis, [(source, source + steps) for source in range(f...  93.1 us
    dot_general x4, matrix products, shards(): jnp.dot(taps, joined[s:s + taps.shape[1]], preferred_element_type=jnp.flo...  37.3 us
    pallas_call x1, Pallas kernels, robust_stack(): pl.pallas_call(functools.partial(stack_kernel, n_tm, n_chan, total_count)...  36.9 us
    unnamed x10, local copies, waits for them, and re-layouts  17.1 us
  transfers between devices with their start and end apart: 2, of which 2 were waited for; matrix products, arithmetic and copies ran while one was open for 6% of the time, Pallas kernels for 1%

profile of v1, /device:TPU:0, one launch (start us, length us, event | category | flops | bytes accessed | tf_op | source)
XLA Modules:
  0.0 328.9 jit_solution(15997618986222634218)
XLA Ops:
  0.0 0.0 copy-start
  0.0 0.0 copy-start.2
  0.0 0.0 copy-start.3
  0.0 5.1 %slice.76 = bf16[1024,2560]{1,0:T(8,128)(2,1)} slice(bf16[3584,2560]{1,0:T(8,128)(2,1)} %param.4), slice={[0:1024], [0:2560]} | slice | bytes 10485760 | tf_op jit(solution)/shard_map/slice | solution.py:292
  5.2 1.3 collective-permute-start
  6.4 0.0 copy-done.2
  6.5 0.1 constant_dynamic-slice_fusion
  6.5 0.5 fusion.22
  9.0 0.0 copy-done.3
  9.1 0.6 reshape.112.pilot_ref
  10.3 4.4 %template.1 = bf16[256,3840]{1,0:T(8,128)(2,1)} custom-call(s32[1]{0:T(128)} %bitcast.1.offset_ref, f32[1,3840]{1,0:T(1,128)} %reshape.112.pilot_ref), custom_call_target="tpu_custom_call" | custom-call | tf_op jit(solution)/shard_map/template/pallas_call | solution.py:42
  14.7 15.6 %constant_dynamic-update-slice_fusion.1 = bf16[4608,2560]{1,0:T(8,128)(2,1)} fusion(bf16[3584,2560]{1,0:T(8,128)(2,1)} %param.4), kind=kLoop, calls=%fused_computation.17 | loop fusion | bytes 36700160
  30.3 0.0 copy-start.1
  30.3 93.1 %collective-permute-done = bf16[1024,2560]{1,0:T(8,128)(2,1)} collective-permute-done((bf16[1024,2560]{1,0:T(8,128)(2,1)}, bf16[1024,2560]{1,0:T(8,128)(2,1)}, u32[]{:S(2)}, u32[]{:S(2)}) %collective-permute-start) | collective-permute-done | bytes 5242912 | tf_op jit(solution)/shard_map/ppermute | solution.py:20
  123.4 5.1 %constant_dynamic-update-slice_fusion = bf16[4608,2560]{1,0:T(8,128)(2,1)} fusion(bf16[4608,2560]{1,0:T(8,128)(2,1)} %constant_dynamic-update-slice_fusion.1, bf16[1024,2560]{1,0:T(8,128)(2,1)} %collective-permute-done), kind=kLoop, calls=%fused_computation.16 | loop fusion | bytes 10485760 | tf_op jit(solution)/shard_map/concatenate | solution.py:293
  128.5 0.0 copy-done.1
  128.5 9.3 %fusion.11 = bf16[256,2560]{1,0:T(8,128)(2,1)S(1)} fusion(bf16[256,3840]{1,0:T(8,128)(2,1)S(1)} %copy-done.1, bf16[4608,2560]{1,0:T(8,128)(2,1)} %constant_dynamic-update-slice_fusion), kind=kOutput, calls=%fused_computation.11 | convolution fusion | flops 5033820160 | bytes 22937600 | tf_op jit(solution)/shard_map/dot_general | solution.py:300
  137.8 9.3 %fusion.14 = bf16[256,2560]{1,0:T(8,128)(2,1)S(1)} fusion(bf16[256,3840]{1,0:T(8,128)(2,1)S(1)} %copy-done.1, bf16[4608,2560]{1,0:T(8,128)(2,1)} %constant_dynamic-update-slice_fusion), kind=kOutput, calls=%fused_computation.12 | convolution fusion | flops 5033820160 | bytes 22937600 | tf_op jit(solution)/shard_map/dot_general | solution.py:300
  147.2 9.3 %fusion.17 = bf16[256,2560]{1,0:T(8,128)(2,1)S(1)} fusion(bf16[256,3840]{1,0:T(8,128)(2,1)S(1)} %copy-done.1, bf16[4608,2560]{1,0:T(8,128)(2,1)} %constant_dynamic-update-slice_fusion), kind=kOutput, calls=%fused_computation.13 | convolution fusion | flops 5033820160 | bytes 22937600 | tf_op jit(solution)/shard_map/dot_general | solution.py:300
  156.5 9.3 %fusion.8 = bf16[256,2560]{1,0:T(8,128)(2,1)S(1)} fusion(bf16[256,3840]{1,0:T(8,128)(2,1)S(1)} %copy-done.1, bf16[4608,2560]{1,0:T(8,128)(2,1)} %constant_dynamic-update-slice_fusion), kind=kOutput, calls=%fused_computation.10 | convolution fusion | flops 5033820160 | bytes 22937600 | tf_op jit(solution)/shard_map/dot_general | solution.py:300
  165.8 3.7 %pad_maximum_fusion = bf16[1024,2560]{1,0:T(8,128)(2,1)} fusion(bf16[256,2560]{1,0:T(8,128)(2,1)S(1)} %fusion.17, bf16[256,2560]{1,0:T(8,128)(2,1)S(1)} %fusion.14, bf16[256,2560]{1,0:T(8,128)(2,1)S(1)} %fusion.11, bf16[256,2560]{1,0:T(8,128)(2,1)S(1)} %fusion.8), kind=kLoop, calls=%fused_computation.9 | loop fusion | flops 20971520 | bytes 10485760 | tf_op jit(solution)/shard_map/concatenate | solution.py:303
  169.6 5.9 %all-to-all-start = ((bf16[8,128,2560]{2,1,0:T(8,128)(2,1)}), bf16[8,128,2560]{2,1,0:T(8,128)(2,1)}, u32[]{:S(2)}, u32[]{:S(2)}) async-start(bf16[8,128,2560]{2,1,0:T(8,128)(2,1)} %bitcast.12), calls=%async_computation | async-start | bytes 10485760 | tf_op jit(solution)/shard_map/all_to_all | solution.py:304
  175.5 0.1 slice.82
  175.6 0.5 slice.83
  176.1 0.1 slice.84
  176.2 0.1 slice.86
  176.3 0.0 copy-done
  176.3 0.6 gather_fusion
  176.9 0.1 fusion.21
  177.0 0.7 add_compare_fusion
  177.7 112.7 %all-to-all-done.traces = bf16[8,128,2560]{2,1,0:T(8,128)(2,1)} async-done(((bf16[8,128,2560]{2,1,0:T(8,128)(2,1)}), bf16[8,128,2560]{2,1,0:T(8,128)(2,1)}, u32[]{:S(2)}, u32[]{:S(2)}) %all-to-all-start) | async-done | bytes 5242912 | tf_op jit(solution)/shard_map/all_to_all | solution.py:304
  290.4 0.1 broadcast_in_dim.10.same
  290.5 0.1 broadcast_in_dim.11.place
  290.5 36.9 %robust_stack.1 = f32[2,128,2560]{2,1,0:T(8,128)S(1)} custom-call(bf16[8,128,2560]{2,1,0:T(8,128)(2,1)} %all-to-all-done.traces, f32[4,8,128]{2,1,0:T(8,128)S(1)} %broadcast_in_dim.10.same, f32[2,8,128]{2,1,0:T(8,128)S(1)} %broadcast_in_dim.11.place), custom_call_target="tpu_custom_call" | custom-call | tf_op jit(solution)/shard_map/robust_stack/pallas_call | solution.py:261
  327.4 1.5 copy.7
  (8 shorter events, 0.0 us)
Async XLA Ops:
  0.0 176.3 %copy-start = (s32[2]{0:T(128)S(1)}, s32[2]{0:T(128)}, u32[]{:S(2)}) copy-start(s32[2]{0:T(128)} %param.7) | copy-start | bytes 28
  0.0 6.4 %copy-start.2 = (s32[3,8]{1,0:T(4,128)S(1)}, s32[3,8]{1,0:T(4,128)}, u32[]{:S(2)}) copy-start(s32[3,8]{1,0:T(4,128)} %param.6) | copy-start | bytes 292
  0.0 9.0 %copy-start.3 = (bf16[3072]{0:T(1024)(128)(2,1)S(1)}, bf16[3072]{0:T(1024)(128)(2,1)}, u32[]{:S(2)}) copy-start(bf16[3072]{0:T(1024)(128)(2,1)} %param.5) | copy-start | bytes 18436
  5.2 118.2 %collective-permute-start = (bf16[1024,2560]{1,0:T(8,128)(2,1)}, bf16[1024,2560]{1,0:T(8,128)(2,1)}, u32[]{:S(2)}, u32[]{:S(2)}) collective-permute-start(bf16[1024,2560]{1,0:T(8,128)(2,1)} %slice.76), channel_id=1, source_target_pairs={{4,0},{8,4},{12,8},{16,12},{20,16},{24,20},{28,24},{5,1},{9,5},{13... | collective-permute-start | bytes 15728648 | tf_op jit(solution)/shard_map/ppermute | solution.py:20
  30.3 98.2 %copy-start.1 = (bf16[256,3840]{1,0:T(8,128)(2,1)S(1)}, bf16[256,3840]{1,0:T(8,128)(2,1)}, u32[]{:S(2)}) copy-start(bf16[256,3840]{1,0:T(8,128)(2,1)} %template.1) | copy-start | bytes 5898244
  169.6 120.8 %all-to-all-start = ((bf16[8,128,2560]{2,1,0:T(8,128)(2,1)}), bf16[8,128,2560]{2,1,0:T(8,128)(2,1)}, u32[]{:S(2)}, u32[]{:S(2)}) async-start(bf16[8,128,2560]{2,1,0:T(8,128)(2,1)} %bitcast.12), calls=%async_computation | async-start | bytes 10485760 | tf_op jit(solution)/shard_map/all_to_all | solution.py:304
